TPU v7x, 32 devices: a whole 2x2x4 slice. The times are simulated.
32 devices in a mesh: groups: 2 (over y), path: 4 (over z), inner: 2 (over x), shard: 2 (over core).
Axes of the slice: x: 2, y: 2, z: 4, core: 2. Of those that a mesh axis runs over, the one named last changes fastest.
Arguments:
- route: int32 [8], P('groups'), parts along dimension 0, may hold values from 0 to 7, as said below
- inputs: bfloat16 [8, 512, 2048], P(('groups', 'path'), 'inner'), parts along dimension 0, may hold values from -6 to 6
- targets: bfloat16 [8, 512, 2048], P(('groups', 'path'), 'inner', 'shard'), parts along dimension 0, may hold values from -6 to 6
- path_weights: bfloat16 [8, 2048, 2048], P(('groups', 'path'), 'inner', 'shard'), parts along dimension 0, may hold values from -6 to 6
- momentum: float32 [16, 2, 1024, 2048], P('groups', 'inner', 'path', 'shard'), parts along dimension 0, may hold values from -2 to 2
Outputs:
- new_weights: bfloat16 [8, 2048, 2048], P(('groups', 'path'), 'inner', 'shard'), parts along dimension 0
- new_momentum: float32 [16, 2, 1024, 2048], P('groups', 'inner', 'path', 'shard'), parts along dimension 0
There are 2 independent parts, one for each index of `groups`. A program takes and returns all parts, laid end to end along the dimension named above; each array names one. Nothing has to cross between parts.
Inputs may be any that keep to these rules, and one draw needn't show every extreme that they name: `route`: where 4 >= 8, every module is used by at least one path; where 4 <= 8, the paths use 4 different modules.
All inputs are finite; a program needn't handle non-finite values.
Results may differ from a plain program's by a relative error of at most 0.0055.
Values may be sent and summed in bfloat16 or wider, within the bound.
A program may use at most 128 MiB of HBM per device.

v0:
```python
import jax
import jax.numpy as jnp
from jax import lax
from jax.sharding import PartitionSpec as P

eps = 1e-06
inner_rate = 256.0
outer_rate = 0.7
outer_mu = 0.9


def per_device(route, inputs, targets, path_weights, momentum):
    n_path = lax.axis_size("path")
    tokens = inputs[0]
    target = targets[0]
    weight = path_weights[0]
    width = tokens.shape[1]
    scale = width ** (-0.5)
    xf = tokens.astype(jnp.float32)
    normed = (xf * lax.rsqrt(jnp.mean(xf * xf, axis=-1, keepdims=True) + eps)).astype(jnp.bfloat16)
    normed_cols = lax.all_to_all(normed, "inner", split_axis=1, concat_axis=0, tiled=True)
    tok_path = normed_cols.shape[0]
    coef = inner_rate * scale / tok_path
    output = jnp.dot(
        normed,
        lax.all_gather(weight, "inner", axis=0, tiled=True),
        preferred_element_type=jnp.float32,
    )
    resid = (output * scale - target.astype(jnp.float32)).astype(jnp.bfloat16)
    grad = lax.dot_general(
        normed_cols,
        lax.all_gather(resid, "inner", axis=0, tiled=True),
        (((0,), (0,)), ((), ())),
        preferred_element_type=jnp.float32,
    )
    delta = (grad * coef).astype(jnp.bfloat16)
    blocks = delta.reshape(n_path, weight.shape[0] // n_path, weight.shape[1])
    received = lax.all_to_all(blocks, "path", split_axis=0, concat_axis=0, tiled=True)
    modules = momentum.shape[0]
    onehot = (route[:, None] == jnp.arange(modules, dtype=jnp.int32)[None, :]).astype(jnp.bfloat16)
    counts = jnp.sum(onehot.astype(jnp.float32), axis=0)
    summed = jnp.einsum("pm,prc->mrc", onehot, received, preferred_element_type=jnp.float32)
    mean_delta = summed / jnp.maximum(counts, 1.0)[:, None, None]
    new_velocity = outer_mu * momentum[:, 0] + mean_delta
    update = (outer_rate * (mean_delta + outer_mu * new_velocity)).astype(jnp.bfloat16)
    outgoing = jnp.einsum("pm,mrc->prc", onehot, update, preferred_element_type=jnp.float32).astype(
        jnp.bfloat16
    )
    returned = lax.all_to_all(outgoing, "path", split_axis=0, concat_axis=0, tiled=True)
    returned = returned.reshape(weight.shape[0], weight.shape[1])
    new_weight = (weight.astype(jnp.float32) - returned.astype(jnp.float32)).astype(jnp.bfloat16)
    return (new_weight[None], new_velocity[:, None])


def solution(mesh):
    placed = (
        P("groups"),
        P(("groups", "path"), "inner", None),
        P(("groups", "path"), "inner", "shard"),
        P(("groups", "path"), "inner", "shard"),
        P("groups", "inner", "path", "shard"),
    )
    return jax.shard_map(
        per_device,
        mesh=mesh,
        in_specs=placed,
        out_specs=(P(("groups", "path"), "inner", "shard"), P("groups", "inner", "path", "shard")),
        check_vma=False,
    )
```

profile of v0, /device:TPU:0, one launch (start us, length us, event | category | flops | bytes accessed | tf_op | source)
XLA Modules:
  0.0 238.8 jit_solution(18421610877471146540)
XLA Ops:
  7.2 0.0 copy-start.3
  7.2 0.0 all-gather.6.cloned.1.call-start
  7.2 0.7 all-gather.6.cloned.1.call-update
  7.9 0.0 all-gather.4.cloned.1.call-start
  8.0 1.5 copy.20
  9.4 0.3 fusion.7
  9.8 59.3 %all-gather.6.cloned.1.call-done = bf16[1,2048,1024]{2,1,0:T(8,128)(2,1)} async-done(((bf16[1,1024,1024]{2,1,0:T(8,128)(2,1)}), bf16[1,2048,1024]{2,1,0:T(8,128)(2,1)}) %all-gather.6.cloned.1.call-update) | async-done | bytes 4194320 | tf_op jit(solution)/shard_map/all_gather | solution.py:26
  69.0 0.0 copy-done.3
  69.0 4.3 %fusion.17 = bf16[256,1024]{1,0:T(8,128)(2,1)} fusion(bf16[1,2048,1024]{2,1,0:T(8,128)(2,1)} %all-gather.6.cloned.1.call-done, bf16[1,256,2048]{1,2,0:T(8,128)(2,1)S(1)} %copy.20, f32[256]{0:T(256)S(1)} %add_rsqrt_fusion, bf16[1,256,1024]{2,1,0:T(8,128)(2,1)S(1)} %copy-done.3), kind=kOutput, calls=%fused_computation.22 | convolution fusion | flops 1076363264 | bytes 6292480 | tf_op jit(solution)/shard_map/dot_general | solution.py:24
  73.3 0.0 all-gather.4.cloned.1.call-update
  73.3 0.2 multiply_convert_fusion.3
  73.5 23.9 %all_to_all.26 = bf16[256,2,1024]{0,2,1:T(8,128)(2,1)S(1)} all-to-all(bf16[256,2,1024]{0,2,1:T(8,128)(2,1)S(1)} %multiply_convert_fusion.3), channel_id=1, replica_groups=mesh['groups'=2,'path'=4,'inner'=2,'shard'=2] {'inner'}, dimensions={1} | all-to-all | bytes 2097152 | tf_op jit(solution)/shard_map/all_to_all | solution.py:21
  97.4 0.5 copy.21
  98.0 3.4 %all-gather.4.cloned.1.call-done = bf16[512,1024]{1,0:T(8,128)(2,1)} async-done(((bf16[256,1024]{1,0:T(8,128)(2,1)}), bf16[512,1024]{1,0:T(8,128)(2,1)}) %all-gather.4.cloned.1.call-update) | async-done | bytes 1048592 | tf_op jit(solution)/shard_map/all_gather | solution.py:32
  101.3 3.8 %multiply_convert_fusion.2 = bf16[1024,1024]{1,0:T(8,128)(2,1)} fusion(bf16[512,1024]{1,0:T(8,128)(2,1)S(1)} %bitcast.49, bf16[512,1024]{1,0:T(8,128)(2,1)} %all-gather.4.cloned.1.call-done), kind=kOutput, calls=%fused_computation.12 | convolution fusion | flops 1075838976 | bytes 4194304 | tf_op jit(solution)/shard_map/dot_general | solution.py:30
  105.2 0.0 copy-start.2
  105.2 4.7 %all-to-all-start.1 = ((bf16[4,256,1024]{2,1,0:T(8,128)(2,1)}), bf16[4,256,1024]{2,1,0:T(8,128)(2,1)S(1)}, u32[]{:S(2)}, u32[]{:S(2)}) async-start(bf16[4,256,1024]{2,1,0:T(8,128)(2,1)} %bitcast.48), calls=%async_computation.1 | async-start | bytes 4194304 | tf_op jit(solution)/shard_map/all_to_all | solution.py:38
  109.9 0.0 copy-done.2
  109.9 0.1 convert_reduce_fusion
  110.0 48.3 %all-to-all-done.1 = bf16[4,256,1024]{2,1,0:T(8,128)(2,1)S(1)} async-done(((bf16[4,256,1024]{2,1,0:T(8,128)(2,1)}), bf16[4,256,1024]{2,1,0:T(8,128)(2,1)S(1)}, u32[]{:S(2)}, u32[]{:S(2)}) %all-to-all-start.1) | async-done | bytes 2097184 | tf_op jit(solution)/shard_map/all_to_all | solution.py:38
  158.3 2.4 %broadcast_divide_fusion = f32[8,256,1024]{2,0,1:T(8,128)S(1)} fusion(f32[8]{0:T(128)S(1)} %broadcast_maximum_fusion, bf16[4,256,1024]{2,1,0:T(8,128)(2,1)S(1)} %all-to-all-done.1, s32[4]{0:T(128)S(1)} %copy-done.2), kind=kOutput, calls=%fused_computation.11 | convolution fusion | flops 18874400 | bytes 10485808 | tf_op jit(solution)/shard_map/pm,prc->mrc/dot_general | solution.py:42
  160.8 0.0 copy-start
  160.8 13.0 %fusion.10 = bf16[4,256,1024]{2,0,1:T(4,128)(2,1)S(1)} fusion(f32[8,256,1024]{2,0,1:T(8,128)S(1)} %broadcast_divide_fusion, f32[8,1,256,1024]{3,2,1,0:T(8,128)} %param.9, s32[4]{0:T(128)S(1)} %copy-done.2), kind=kOutput, calls=%fused_computation.19 | convolution fusion | flops 30408736 | bytes 18874384 | tf_op jit(solution)/shard_map/pm,mrc->prc/dot_general | solution.py:46
  173.8 0.0 copy-done
  173.8 1.9 copy.24
  175.8 4.7 %all-to-all-start.2 = ((bf16[4,256,1024]{2,1,0:T(8,128)(2,1)}), bf16[4,256,1024]{2,1,0:T(8,128)(2,1)}, u32[]{:S(2)}, u32[]{:S(2)}) async-start(bf16[4,256,1024]{2,1,0:T(8,128)(2,1)} %copy.24), calls=%async_computation.2 | async-start | bytes 4194304 | tf_op jit(solution)/shard_map/all_to_all | solution.py:49
  180.5 14.9 %fusion.6 = f32[8,1,256,1024]{3,0,2,1:T(8,128)} fusion(f32[8,256,1024]{2,0,1:T(8,128)} %copy-done, f32[8,1,256,1024]{3,2,1,0:T(8,128)} %param.9), kind=kLoop, calls=%fused_computation.10 | loop fusion | flops 4194304 | bytes 25165824 | tf_op jit(solution)/shard_map/broadcast_in_dim | solution.py:52
  195.4 0.0 copy-start.1
  195.4 11.8 %copy.25 = f32[8,1,256,1024]{3,2,1,0:T(8,128)} copy(f32[8,1,256,1024]{3,0,2,1:T(8,128)} %fusion.6) | data formatting | bytes 16777216
  207.2 20.9 %all-to-all-done.2 = bf16[4,256,1024]{2,1,0:T(8,128)(2,1)} async-done(((bf16[4,256,1024]{2,1,0:T(8,128)(2,1)}), bf16[4,256,1024]{2,1,0:T(8,128)(2,1)}, u32[]{:S(2)}, u32[]{:S(2)}) %all-to-all-start.2) | async-done | bytes 2097184 | tf_op jit(solution)/shard_map/all_to_all | solution.py:49
  228.1 0.0 copy-done.1
  228.1 3.9 %fusion.1 = bf16[1,1024,1024]{2,1,0:T(8,128)(2,1)} fusion(bf16[1,1024,1024]{2,1,0:T(8,128)(2,1)S(1)} %copy-done.1, bf16[1,1024,1024]{2,1,0:T(8,128)(2,1)} %bitcast.45), kind=kLoop, calls=%fused_computation.5 | loop fusion | flops 4194304 | bytes 6291456 | tf_op jit(solution)/shard_map/convert_element_type | solution.py:51
  (2 shorter events, 0.0 us)
Async XLA Ops:
  7.2 61.9 %copy-start.3 = (bf16[1,256,1024]{2,1,0:T(8,128)(2,1)S(1)}, bf16[1,256,1024]{2,1,0:T(8,128)(2,1)}, u32[]{:S(2)}) copy-start(bf16[1,256,1024]{2,1,0:T(8,128)(2,1)} %param.7) | copy-start | bytes 1572868
  7.2 61.9 %all-gather.6.cloned.1.call-start = ((), (), s32[]{:S(2)}) async-start(), calls=%async_computation.4 | async-start | bytes 6291456 | tf_op jit(solution)/shard_map/all_gather | solution.py:26
  7.9 93.4 %all-gather.4.cloned.1.call-start = ((), (), s32[]{:S(2)}) async-start(), calls=%async_computation.3 | async-start | bytes 1572864 | tf_op jit(solution)/shard_map/all_gather | solution.py:32
  105.2 4.7 %copy-start.2 = (s32[4]{0:T(128)S(1)}, s32[4]{0:T(128)}, u32[]{:S(2)}) copy-start(s32[4]{0:T(128)} %param.5) | copy-start | bytes 52
  105.2 53.2 %all-to-all-start.1 = ((bf16[4,256,1024]{2,1,0:T(8,128)(2,1)}), bf16[4,256,1024]{2,1,0:T(8,128)(2,1)S(1)}, u32[]{:S(2)}, u32[]{:S(2)}) async-start(bf16[4,256,1024]{2,1,0:T(8,128)(2,1)} %bitcast.48), calls=%async_computation.1 | async-start | bytes 4194304 | tf_op jit(solution)/shard_map/all_to_all | solution.py:38
  160.8 13.0 %copy-start = (f32[8,256,1024]{2,0,1:T(8,128)}, f32[8,256,1024]{2,0,1:T(8,128)S(1)}, u32[]{:S(2)}) copy-start(f32[8,256,1024]{2,0,1:T(8,128)S(1)} %broadcast_divide_fusion) | copy-start | bytes 25165828
  175.8 52.3 %all-to-all-start.2 = ((bf16[4,256,1024]{2,1,0:T(8,128)(2,1)}), bf16[4,256,1024]{2,1,0:T(8,128)(2,1)}, u32[]{:S(2)}, u32[]{:S(2)}) async-start(bf16[4,256,1024]{2,1,0:T(8,128)(2,1)} %copy.24), calls=%async_computation.2 | async-start | bytes 4194304 | tf_op jit(solution)/shard_map/all_to_all | solution.py:49
  195.4 32.6 %copy-start.1 = (bf16[1,1024,1024]{2,1,0:T(8,128)(2,1)S(1)}, bf16[1,1024,1024]{2,1,0:T(8,128)(2,1)}, u32[]{:S(2)}) copy-start(bf16[1,1024,1024]{2,1,0:T(8,128)(2,1)} %param.8) | copy-start | bytes 6291460
Sparse Core Ops, SparseCore 0:
  9.6 59.4 all-gather.5
  73.4 27.8 all-gather.3
where the time goes:
time: 239 us
  waiting for transfers between devices  133 us (56%)
  blocking collectives  23.9 us (10%)
  matrix products  23.6 us (10%)
  other arithmetic  19.4 us (8%)
  local copies, waits for them, and re-layouts  15.8 us (7%)
  between operations  14.1 us (6%)
  starting transfers between devices  9.52 us (4%)
    all_gather x1, waiting for transfers between devices, per_device(): lax.all_gather(weight, 'inner', axis=0, tiled=True)  59.3 us
    all_to_all x1, waiting for transfers between devices, per_device(): lax.all_to_all(blocks, 'path', split_axis=0, concat_axis=0, tiled=True)  48.3 us
    all_to_all x1, blocking collectives, per_device(): lax.all_to_all(normed, 'inner', split_axis=1, concat_axis=0, tiled=True)  23.9 us
    all_to_all x1, waiting for transfers between devices, per_device(): lax.all_to_all(outgoing, 'path', split_axis=0, concat_axis=0, tiled=True)  20.9 us
    broadcast_in_dim x1, other arithmetic, per_device(): return (new_weight[None], new_velocity[:, None])  14.9 us
    unnamed x10, local copies, waits for them, and re-layouts  13.3 us
    dot_general x1, matrix products, per_device(): jnp.einsum('pm,mrc->prc', onehot, update, preferred_element_type=jnp.floa...  13 us
  transfers between devices with their start and end apart: 4, of which 4 were waited for; matrix products, arithmetic and copies ran while one was open for 12% of the time, Pallas kernels for 0%

commit v1 on v0

--- a/solution.py
+++ b/solution.py
@@ -1,6 +1,10 @@
+import functools
+
 import jax
 import jax.numpy as jnp
 from jax import lax
+from jax.experimental import pallas as pl
+from jax.experimental.pallas import tpu as pltpu
 from jax.sharding import PartitionSpec as P
 
 eps = 1e-06
@@ -52,6 +56,305 @@
     return (new_weight[None], new_velocity[:, None])
 
 
+def select_kernel(route_ref, momentum_ref, out_ref):
+    out_ref[...] = momentum_ref[...].astype(out_ref.dtype)
+
+
+def select_momentum(route, momentum):
+    n_path = route.shape[0]
+    _, rows, cols = momentum.shape
+    return pl.pallas_call(
+        select_kernel,
+        out_shape=jax.ShapeDtypeStruct((n_path, rows, cols), jnp.bfloat16),
+        grid_spec=pltpu.PrefetchScalarGridSpec(
+            num_scalar_prefetch=1,
+            grid=(n_path,),
+            in_specs=[pl.BlockSpec((1, rows, cols), lambda p, route: (route[p], 0, 0))],
+            out_specs=pl.BlockSpec((1, rows, cols), lambda p, route: (p, 0, 0)),
+        ),
+        compiler_params=pltpu.CompilerParams(vmem_limit_bytes=32 * 2**20),
+        cost_estimate=pl.CostEstimate(flops=0, bytes_accessed=n_path * rows * cols * 6, transcendentals=0),
+    )(route, momentum)
+
+
+def momentum_kernel(slot_ref, used_ref, momentum_ref, delta_ref, out_ref):
+    used = used_ref[pl.program_id(0)]
+
+    @pl.when(used != 0)
+    def _():
+        out_ref[...] = outer_mu * momentum_ref[...] + delta_ref[...].astype(jnp.float32)
+
+    @pl.when(used == 0)
+    def _():
+        out_ref[...] = outer_mu * momentum_ref[...]
+
+
+def next_momentum(route, momentum, received):
+    modules, rows, cols = momentum.shape
+    hit = route[:, None] == jnp.arange(modules, dtype=jnp.int32)[None, :]
+    used = jnp.any(hit, axis=0).astype(jnp.int32)
+    slot = jnp.argmax(hit, axis=0).astype(jnp.int32)
+    return pl.pallas_call(
+        momentum_kernel,
+        out_shape=jax.ShapeDtypeStruct((modules, rows, cols), jnp.float32),
+        grid_spec=pltpu.PrefetchScalarGridSpec(
+            num_scalar_prefetch=2,
+            grid=(modules,),
+            in_specs=[
+                pl.BlockSpec((1, rows, cols), lambda m, slot, used: (m, 0, 0)),
+                pl.BlockSpec((1, rows, cols), lambda m, slot, used: (slot[m], 0, 0)),
+            ],
+            out_specs=pl.BlockSpec((1, rows, cols), lambda m, slot, used: (m, 0, 0)),
+        ),
+        compiler_params=pltpu.CompilerParams(vmem_limit_bytes=32 * 2**20),
+        cost_estimate=pl.CostEstimate(flops=0, bytes_accessed=modules * rows * cols * 9, transcendentals=0),
+    )(slot, used, momentum, received)
+
+
+def sync_kernel(
+    n_path,
+    chunks,
+    x_hbm,
+    t_hbm,
+    w_hbm,
+    m_hbm,
+    new_w_hbm,
+    recv_hbm,
+    x_v,
+    t_v,
+    w_v,
+    nsend,
+    ncols,
+    psend,
+    precv,
+    lp,
+    resid,
+    delta,
+    mom,
+    load_sem,
+    out_sem,
+    x_send,
+    x_recv,
+    m_send,
+    m_recv,
+    d_send,
+    d_recv,
+):
+    f32 = jnp.float32
+    tokens, width = x_v.shape
+    rows, cols = w_v.shape
+    block = rows // n_path
+    step = tokens // chunks
+    tile = min(256, cols)
+    scale = width ** (-0.5)
+    coef = inner_rate * scale / (2 * tokens)
+    me = lax.axis_index("path")
+    mine = lax.axis_index("inner")
+    other = 1 - mine
+
+    load_x = pltpu.make_async_copy(x_hbm, x_v, load_sem.at[0])
+    load_w = pltpu.make_async_copy(w_hbm, w_v, load_sem.at[1])
+    load_t = pltpu.make_async_copy(t_hbm, t_v, load_sem.at[2])
+    load_m = pltpu.make_async_copy(m_hbm.at[me], mom.at[me], load_sem.at[3])
+    load_x.start()
+    load_w.start()
+    load_t.start()
+    load_m.start()
+
+    barrier = pltpu.get_barrier_semaphore()
+    pl.semaphore_signal(barrier, inc=1, device_id={"inner": other}, device_id_type=pl.DeviceIdType.MESH)
+    for d in range(1, n_path):
+        pl.semaphore_signal(
+            barrier, inc=1, device_id={"path": lax.rem(me + d, n_path)}, device_id_type=pl.DeviceIdType.MESH
+        )
+    pl.semaphore_wait(barrier, n_path)
+
+    def far(d, src, dst, send, recv):
+        return pltpu.make_async_remote_copy(
+            src_ref=src,
+            dst_ref=dst,
+            send_sem=send.at[d - 1],
+            recv_sem=recv.at[d - 1],
+            device_id={"path": lax.rem(me + d, n_path)},
+            device_id_type=pl.DeviceIdType.MESH,
+        )
+
+    def near(hop, c, src, dst):
+        return pltpu.make_async_remote_copy(
+            src_ref=src,
+            dst_ref=dst,
+            send_sem=x_send.at[hop, c],
+            recv_sem=x_recv.at[hop, c],
+            device_id={"inner": other},
+            device_id_type=pl.DeviceIdType.MESH,
+        )
+
+    mom_copies = [far(d, m_hbm.at[lax.rem(me + d, n_path)], mom.at[me], m_send, m_recv) for d in range(1, n_path)]
+    for copy in mom_copies:
+        copy.start()
+
+    load_x.wait()
+    piece = 32
+    own_at = pl.ds(pl.multiple_of(mine * rows, rows), rows)
+    other_at = pl.ds(pl.multiple_of(other * rows, rows), rows)
+    hop0 = []
+    for c in range(chunks):
+
+        @pl.loop(0, step // piece)
+        def _(k, c=c):
+            at = pl.ds(pl.multiple_of(c * step + k * piece, piece), piece)
+            xf = x_v[at, :].astype(f32)
+            inv = lax.rsqrt(jnp.mean(xf * xf, axis=-1, keepdims=True) + eps)
+            ncols[at, :] = (x_v[at, own_at].astype(f32) * inv).astype(jnp.bfloat16)
+            nsend[at, :] = (x_v[at, other_at].astype(f32) * inv).astype(jnp.bfloat16)
+
+        at = pl.ds(c * step, step)
+        copy = near(0, c, nsend.at[at], ncols.at[pl.ds(tokens + c * step, step)])
+        copy.start()
+        hop0.append(copy)
+
+    load_w.wait()
+    load_t.wait()
+
+    @pl.loop(0, cols // tile)
+    def _(j):
+        at = pl.ds(pl.multiple_of(j * tile, tile), tile)
+        part = jnp.dot(ncols[0:tokens, :], w_v[:, at], preferred_element_type=f32)
+        lp[:, at] = part * scale - t_v[:, at].astype(f32)
+
+    hop1 = []
+    for c in range(chunks):
+        hop0[c].wait_recv()
+
+        @pl.loop(0, cols // tile)
+        def _(j, c=c):
+            at = pl.ds(pl.multiple_of(j * tile, tile), tile)
+            part = jnp.dot(
+                ncols[tokens + c * step : tokens + (c + 1) * step, :], w_v[:, at], preferred_element_type=f32
+            )
+            psend[c * step : (c + 1) * step, at] = (part * scale).astype(jnp.bfloat16)
+
+        at = pl.ds(c * step, step)
+        copy = near(1, c, psend.at[at], precv.at[at])
+        copy.start()
+        hop1.append(copy)
+
+    hop2 = []
+    for c in range(chunks):
+        hop1[c].wait_recv()
+
+        @pl.loop(0, step // piece)
+        def _(k, c=c):
+            at = pl.ds(pl.multiple_of(c * step + k * piece, piece), piece)
+            resid[at, :] = (lp[at, :] + precv[at, :].astype(f32)).astype(jnp.bfloat16)
+
+        copy = near(2, c, resid.at[pl.ds(c * step, step)], resid.at[pl.ds(tokens + c * step, step)])
+        copy.start()
+        hop2.append(copy)
+    for copy in hop2:
+        copy.wait_recv()
+
+    delta_copies = []
+    for d in list(range(1, n_path)) + [0]:
+        q = lax.rem(me + d, n_path)
+        left = pl.ds(pl.multiple_of(q * block, block), block)
+
+        @pl.loop(0, cols // tile)
+        def _(j, q=q, left=left):
+            at = pl.ds(pl.multiple_of(j * tile, tile), tile)
+            grad = lax.dot_general(
+                ncols[:, left], resid[:, at], (((0,), (0,)), ((), ())), preferred_element_type=f32
+            )
+            delta[q, :, at] = (grad * coef).astype(jnp.bfloat16)
+
+        if d > 0:
+            copy = far(d, delta.at[q], recv_hbm.at[me], d_send, d_recv)
+        else:
+            copy = pltpu.make_async_copy(delta.at[q], recv_hbm.at[me], out_sem.at[0])
+        copy.start()
+        delta_copies.append(copy)
+
+    out_copies = []
+    for d in range(n_path):
+        if d == 0:
+            load_m.wait()
+        else:
+            mom_copies[d - 1].wait_recv()
+        o = lax.rem(me + n_path - d, n_path)
+
+        @pl.loop(0, block // piece)
+        def _(k, o=o):
+            at = pl.ds(pl.multiple_of(k * piece, piece), piece)
+            w_at = pl.ds(pl.multiple_of(o * block + k * piece, piece), piece)
+            step_delta = delta[o, at, :].astype(f32)
+            velocity = outer_mu * mom[o, at, :].astype(f32) + step_delta
+            update = (outer_rate * (step_delta + outer_mu * velocity)).astype(jnp.bfloat16)
+            w_v[w_at, :] = (w_v[w_at, :].astype(f32) - update.astype(f32)).astype(jnp.bfloat16)
+
+        here = pl.ds(pl.multiple_of(o * block, block), block)
+        copy = pltpu.make_async_copy(w_v.at[here], new_w_hbm.at[here], out_sem.at[1 + d])
+        copy.start()
+        out_copies.append(copy)
+
+    for copy in hop0 + hop1 + hop2 + mom_copies:
+        copy.wait_send()
+    for copy in delta_copies[:-1]:
+        copy.wait()
+    delta_copies[-1].wait()
+    for copy in out_copies:
+        copy.wait()
+
+
+def distinct_device(route, inputs, targets, path_weights, momentum):
+    n_path = lax.axis_size("path")
+    tokens, width = inputs.shape[1:]
+    rows, cols = path_weights.shape[1:]
+    block = rows // n_path
+    chunks = 2
+    bf16 = jnp.bfloat16
+    held = momentum[:, 0]
+    outgoing = select_momentum(route, held)
+    any_space = pl.BlockSpec(memory_space=pl.ANY)
+    dma = pltpu.SemaphoreType.DMA
+    new_weight, received = pl.pallas_call(
+        functools.partial(sync_kernel, n_path, chunks),
+        out_shape=(
+            jax.ShapeDtypeStruct((rows, cols), bf16),
+            jax.ShapeDtypeStruct((n_path, block, cols), bf16),
+        ),
+        in_specs=[any_space] * 4,
+        out_specs=(any_space, any_space),
+        scratch_shapes=[
+            pltpu.VMEM((tokens, width), bf16),
+            pltpu.VMEM((tokens, cols), bf16),
+            pltpu.VMEM((rows, cols), bf16),
+            pltpu.VMEM((tokens, rows), bf16),
+            pltpu.VMEM((2 * tokens, rows), bf16),
+            pltpu.VMEM((tokens, cols), bf16),
+            pltpu.VMEM((tokens, cols), bf16),
+            pltpu.VMEM((tokens, cols), jnp.float32),
+            pltpu.VMEM((2 * tokens, cols), bf16),
+            pltpu.VMEM((n_path, block, cols), bf16),
+            pltpu.VMEM((n_path, block, cols), bf16),
+            dma((4,)),
+            dma((1 + n_path,)),
+            dma((3, chunks)),
+            dma((3, chunks)),
+            dma((n_path - 1,)),
+            dma((n_path - 1,)),
+            dma((n_path - 1,)),
+            dma((n_path - 1,)),
+        ],
+        compiler_params=pltpu.CompilerParams(
+            collective_id=0, has_side_effects=True, vmem_limit_bytes=48 * 2**20
+        ),
+        cost_estimate=pl.CostEstimate(
+            flops=8 * tokens * rows * cols, bytes_accessed=12 * rows * cols, transcendentals=0
+        ),
+    )(inputs[0], targets[0], path_weights[0], outgoing)
+    return (new_weight[None], next_momentum(route, held, received)[:, None])
+
+
 def solution(mesh):
     placed = (
         P("groups"),
@@ -60,8 +363,14 @@
         P(("groups", "path"), "inner", "shard"),
         P("groups", "inner", "path", "shard"),
     )
+
+    def step(route, inputs, targets, path_weights, momentum):
+        paths, modules = mesh.shape["path"], momentum.shape[0]
+        distinct = 2 <= paths <= modules and mesh.shape["inner"] == 2
+        return (distinct_device if distinct else per_device)(route, inputs, targets, path_weights, momentum)
+
     return jax.shard_map(
-        per_device,
+        step,
         mesh=mesh,
         in_specs=placed,
         out_specs=(P(("groups", "path"), "inner", "shard"), P("groups", "inner", "path", "shard")),

time: 239 us -> 110 us (0.46)
  the two profiles are of different devices: /device:TPU:0 before, /device:TPU:8 now
where the time goes in v1:
time: 110 us; the launch traced here: 109 us
  Pallas kernels  100 us (91%)
  local copies, waits for them, and re-layouts  6.68 us (6%)
  other arithmetic  2.01 us (2%)
    pallas_call x1, Pallas kernels, distinct_device(): pl.pallas_call(functools.partial(sync_kernel, n_path, chunks), out_shape=...  94.1 us
    unnamed x13, local copies, waits for them, and re-layouts  6.68 us
    pallas_call x1, Pallas kernels, next_momentum(): pl.pallas_call(momentum_kernel, out_shape=jax.ShapeDtypeStruct((modules,...  5.18 us

profile of v1, /device:TPU:8, one launch (start us, length us, event | category | flops | bytes accessed | tf_op | source)
XLA Modules:
  0.0 109.5 jit_solution(1907700997328388548)
XLA Ops:
  0.6 0.7 fusion
  1.4 1.3 %iota_reduce_fusion = (pred[8]{0:T(512)(128)(4,1)}, s32[8]{0:T(128)S(1)}) fusion(s32[4]{0:T(128)} %route_ref.1), kind=kLoop, calls=%fused_computation | loop fusion | flops 200 | bytes 56 | tf_op jit(solution)/shard_map/next_momentum/reduce | solution.py:96
  2.6 0.0 copy-start
  2.6 3.4 %copy-done = f32[8,1,256,1024]{3,2,1,0:T(8,128)S(1)} copy-done((f32[8,1,256,1024]{3,2,1,0:T(8,128)S(1)}, f32[8,1,256,1024]{3,2,1,0:T(8,128)}, u32[]{:S(2)}) %copy-start) | copy-done | bytes 8388632
  6.0 0.0 copy-start.3
  6.0 0.7 copy-done.3
  6.7 0.0 copy-start.4
  6.7 0.0 copy-start.5
  6.7 0.0 copy-start.1
  6.7 0.8 shard_map.68.m_hbm
  7.5 0.0 copy-start.2
  7.5 1.3 %copy-done.2 = bf16[4,256,1024]{2,1,0:T(8,128)(2,1)} copy-done((bf16[4,256,1024]{2,1,0:T(8,128)(2,1)}, bf16[4,256,1024]{2,1,0:T(8,128)(2,1)S(1)}, u32[]{:S(2)}) %copy-start.2) | copy-done | bytes 2097176
  8.8 0.0 copy-done.4
  8.8 0.0 copy-done.5
  8.8 94.1 %shard_map.69 = (bf16[1024,1024]{1,0:T(8,128)(2,1)S(1)}, bf16[4,256,1024]{2,1,0:T(8,128)(2,1)S(1)}) custom-call(bf16[256,2048]{1,0:T(8,128)(2,1)S(1)} %bitcast.11, bf16[256,1024]{1,0:T(8,128)(2,1)S(1)} %bitcast.12, bf16[1024,1024]{1,0:T(8,128)(2,1)} %bitcast.14, bf16[4,256,1024]{2,1,0:T(8,128)(2,1)} %copy-done.2), custom_call_target="tpu_custom_call" | custom-call | flops 2147483648 | bytes 12582912 | tf_op jit(solution)/shard_map/pallas_call | solution.py:319
  103.0 0.0 copy-done.1
  103.0 5.2 %shard_map.70 = f32[8,256,1024]{2,1,0:T(8,128)} custom-call(s32[8]{0:T(128)S(1)} %get-tuple-element.6.slot_ref, s32[8]{0:T(128)S(1)} %convert_element_type.3.used_ref, f32[8,256,1024]{2,1,0:T(8,128)S(1)} %bitcast.9, bf16[4,256,1024]{2,1,0:T(8,128)(2,1)S(1)} %get-tuple-element.7.delta_ref), custom_call_target="tpu_custom_call" | custom-call | bytes 18874368 | tf_op jit(solution)/shard_map/pallas_call | solution.py:97
  108.2 1.3 %copy.10 = bf16[1,1024,1024]{2,1,0:T(8,128)(2,1)} copy(bf16[1,1024,1024]{2,1,0:T(8,128)(2,1)S(1)} %bitcast.10) | data formatting | bytes 4194304
  (1 shorter events, 0.0 us)
Async XLA Ops:
  2.6 3.4 %copy-start = (f32[8,1,256,1024]{3,2,1,0:T(8,128)S(1)}, f32[8,1,256,1024]{3,2,1,0:T(8,128)}, u32[]{:S(2)}) copy-start(f32[8,1,256,1024]{3,2,1,0:T(8,128)} %param.9) | copy-start | bytes 25165828
  6.0 0.7 copy-start.3
  6.7 2.2 %copy-start.4 = (bf16[1,256,2048]{2,1,0:T(8,128)(2,1)S(1)}, bf16[1,256,2048]{2,1,0:T(8,128)(2,1)}, u32[]{:S(2)}) copy-start(bf16[1,256,2048]{2,1,0:T(8,128)(2,1)} %param.6) | copy-start | bytes 3145732
  6.7 2.2 %copy-start.5 = (bf16[1,256,1024]{2,1,0:T(8,128)(2,1)S(1)}, bf16[1,256,1024]{2,1,0:T(8,128)(2,1)}, u32[]{:S(2)}) copy-start(bf16[1,256,1024]{2,1,0:T(8,128)(2,1)} %param.7) | copy-start | bytes 1572868
  6.7 96.3 %copy-start.1 = (f32[8,1,256,1024]{3,2,1,0:T(8,128)S(1)}, f32[8,1,256,1024]{3,2,1,0:T(8,128)}, u32[]{:S(2)}) copy-start(f32[8,1,256,1024]{3,2,1,0:T(8,128)} %param.9) | copy-start | bytes 25165828
  7.5 1.3 %copy-start.2 = (bf16[4,256,1024]{2,1,0:T(8,128)(2,1)}, bf16[4,256,1024]{2,1,0:T(8,128)(2,1)S(1)}, u32[]{:S(2)}) copy-start(bf16[4,256,1024]{2,1,0:T(8,128)(2,1)S(1)} %shard_map.68.m_hbm) | copy-start | bytes 6291460

commit v2 on v1

--- a/solution.py
+++ b/solution.py
@@ -56,29 +56,49 @@
     return (new_weight[None], new_velocity[:, None])
 
 
-def select_kernel(route_ref, momentum_ref, out_ref):
+def select_kernel(route_ref, momentum_ref, out_ref, slot_ref, used_ref):
+    @pl.when(pl.program_id(0) == 0)
+    def _():
+        slot = jnp.int32(0)
+        for m in range(slot_ref.shape[0]):
+            used = jnp.int32(0)
+            for p in range(route_ref.shape[0]):
+                hit = route_ref[p] == m
+                slot = jnp.where(hit, p, slot)
+                used = jnp.where(hit, 1, used)
+            slot_ref[m] = slot
+            used_ref[m] = used
+
     out_ref[...] = momentum_ref[...].astype(out_ref.dtype)
 
 
 def select_momentum(route, momentum):
     n_path = route.shape[0]
-    _, rows, cols = momentum.shape
+    modules, rows, cols = momentum.shape
+    table = jax.ShapeDtypeStruct((modules,), jnp.int32)
+    scalars = pl.BlockSpec(memory_space=pltpu.SMEM)
     return pl.pallas_call(
         select_kernel,
-        out_shape=jax.ShapeDtypeStruct((n_path, rows, cols), jnp.bfloat16),
+        out_shape=(jax.ShapeDtypeStruct((n_path, rows, cols), jnp.bfloat16), table, table),
         grid_spec=pltpu.PrefetchScalarGridSpec(
             num_scalar_prefetch=1,
             grid=(n_path,),
             in_specs=[pl.BlockSpec((1, rows, cols), lambda p, route: (route[p], 0, 0))],
-            out_specs=pl.BlockSpec((1, rows, cols), lambda p, route: (p, 0, 0)),
-        ),
-        compiler_params=pltpu.CompilerParams(vmem_limit_bytes=32 * 2**20),
+            out_specs=(pl.BlockSpec((1, rows, cols), lambda p, route: (p, 0, 0)), scalars, scalars),
+        ),
+        compiler_params=pltpu.CompilerParams(vmem_limit_bytes=57 * 2**20),
         cost_estimate=pl.CostEstimate(flops=0, bytes_accessed=n_path * rows * cols * 6, transcendentals=0),
     )(route, momentum)
 
 
-def momentum_kernel(slot_ref, used_ref, momentum_ref, delta_ref, out_ref):
-    used = used_ref[pl.program_id(0)]
+def momentum_kernel(slot_ref, used_ref, momentum_ref, delta_ref, weight_ref, out_ref, new_weight_ref, sem):
+    m = pl.program_id(0)
+    used = used_ref[m]
+    handed = pltpu.make_async_copy(weight_ref, new_weight_ref, sem)
+
+    @pl.when(m == 0)
+    def _():
+        handed.start()
 
     @pl.when(used != 0)
     def _():
@@ -88,27 +108,36 @@
     def _():
         out_ref[...] = outer_mu * momentum_ref[...]
 
-
-def next_momentum(route, momentum, received):
+    @pl.when(m == pl.num_programs(0) - 1)
+    def _():
+        handed.wait()
+
+
+def next_momentum(slot, used, momentum, received, new_weight):
     modules, rows, cols = momentum.shape
-    hit = route[:, None] == jnp.arange(modules, dtype=jnp.int32)[None, :]
-    used = jnp.any(hit, axis=0).astype(jnp.int32)
-    slot = jnp.argmax(hit, axis=0).astype(jnp.int32)
     return pl.pallas_call(
         momentum_kernel,
-        out_shape=jax.ShapeDtypeStruct((modules, rows, cols), jnp.float32),
+        out_shape=(
+            jax.ShapeDtypeStruct((modules, rows, cols), jnp.float32),
+            jax.ShapeDtypeStruct(new_weight.shape, new_weight.dtype),
+        ),
         grid_spec=pltpu.PrefetchScalarGridSpec(
             num_scalar_prefetch=2,
             grid=(modules,),
             in_specs=[
                 pl.BlockSpec((1, rows, cols), lambda m, slot, used: (m, 0, 0)),
                 pl.BlockSpec((1, rows, cols), lambda m, slot, used: (slot[m], 0, 0)),
+                pl.BlockSpec(memory_space=pl.ANY),
             ],
-            out_specs=pl.BlockSpec((1, rows, cols), lambda m, slot, used: (m, 0, 0)),
-        ),
-        compiler_params=pltpu.CompilerParams(vmem_limit_bytes=32 * 2**20),
+            out_specs=(
+                pl.BlockSpec((1, rows, cols), lambda m, slot, used: (m, 0, 0)),
+                pl.BlockSpec(memory_space=pl.ANY),
+            ),
+            scratch_shapes=[pltpu.SemaphoreType.DMA],
+        ),
+        compiler_params=pltpu.CompilerParams(vmem_limit_bytes=57 * 2**20),
         cost_estimate=pl.CostEstimate(flops=0, bytes_accessed=modules * rows * cols * 9, transcendentals=0),
-    )(slot, used, momentum, received)
+    )(slot, used, momentum, received, new_weight)
 
 
 def sync_kernel(
@@ -313,7 +342,7 @@
     chunks = 2
     bf16 = jnp.bfloat16
     held = momentum[:, 0]
-    outgoing = select_momentum(route, held)
+    outgoing, slot, used = select_momentum(route, held)
     any_space = pl.BlockSpec(memory_space=pl.ANY)
     dma = pltpu.SemaphoreType.DMA
     new_weight, received = pl.pallas_call(
@@ -322,7 +351,7 @@
             jax.ShapeDtypeStruct((rows, cols), bf16),
             jax.ShapeDtypeStruct((n_path, block, cols), bf16),
         ),
-        in_specs=[any_space] * 4,
+        in_specs=[pl.BlockSpec(memory_space=pltpu.HBM)] * 3 + [any_space],
         out_specs=(any_space, any_space),
         scratch_shapes=[
             pltpu.VMEM((tokens, width), bf16),
@@ -352,7 +381,8 @@
             flops=8 * tokens * rows * cols, bytes_accessed=12 * rows * cols, transcendentals=0
         ),
     )(inputs[0], targets[0], path_weights[0], outgoing)
-    return (new_weight[None], next_momentum(route, held, received)[:, None])
+    velocity, new_weight = next_momentum(slot, used, held, received, new_weight)
+    return (new_weight[None], velocity[:, None])
 
 
 def solution(mesh):

time: 110 us -> 171 us (1.55)
  Pallas kernels: 100 us -> 167 us
  local copies, waits for them, and re-layouts: 6.68 us -> 2.67 us
  other arithmetic: 2.01 us -> 0 us
    pallas_call x2, Pallas kernels: 6 us -> 72.7 us  [the longest x1 67.6 us: next_momentum(): pl.pallas_call(momentum_kernel, out_shape=(jax.ShapeDtypeStruct((modules,...]
    unnamed x13 -> x8, local copies, waits for them, and re-layouts: 6.68 us -> 2.67 us
where the time goes in v2:
time: 171 us; the launch traced here: 170 us
  Pallas kernels  167 us (98%)
  local copies, waits for them, and re-layouts  2.67 us (2%)
    pallas_call x1, Pallas kernels, distinct_device(): pl.pallas_call(functools.partial(sync_kernel, n_path, chunks), out_shape=...  94.2 us
    pallas_call x1, Pallas kernels, next_momentum(): pl.pallas_call(momentum_kernel, out_shape=(jax.ShapeDtypeStruct((modules,...  67.6 us
    pallas_call x1, Pallas kernels, select_momentum(): pl.pallas_call(select_kernel, out_shape=(jax.ShapeDtypeStruct((n_path, ro...  5.03 us

profile of v2, /device:TPU:8, one launch (start us, length us, event | category | flops | bytes accessed | tf_op | source)
XLA Modules:
  0.0 170.2 jit_solution(3466375380084361887)
XLA Ops:
  0.6 0.0 copy-start.2
  0.6 0.0 copy-start.3
  0.6 5.0 %shard_map.68 = (bf16[4,256,1024]{2,1,0:T(8,128)(2,1)}, s32[8]{0:T(128)}, s32[8]{0:T(128)}) custom-call(s32[4]{0:T(128)} %route_ref.1, f32[8,256,1024]{2,1,0:T(8,128)} %bitcast.10), custom_call_target="tpu_custom_call" | custom-call | bytes 6291456 | tf_op jit(solution)/shard_map/pallas_call | solution.py:80
  5.7 0.0 copy-done.2
  5.7 0.0 copy-done.3
  5.7 94.2 %shard_map.69 = (bf16[1024,1024]{1,0:T(8,128)(2,1)S(1)}, bf16[4,256,1024]{2,1,0:T(8,128)(2,1)S(1)}) custom-call(bf16[256,2048]{1,0:T(8,128)(2,1)S(1)} %bitcast.8, bf16[256,1024]{1,0:T(8,128)(2,1)S(1)} %bitcast.9, bf16[1024,1024]{1,0:T(8,128)(2,1)} %bitcast.13, bf16[4,256,1024]{2,1,0:T(8,128)(2,1)} %get-tuple-element.11.m_hbm), custom_call_target="tpu_custom_call" | custom-call | flops 2147483648 | bytes 12582912 | tf_op jit(solution)/shard_map/pallas_call | solution.py:348
  99.9 0.0 copy-start
  99.9 1.3 copy-done
  101.2 0.0 copy-start.1
  101.2 1.4 copy-done.1
  102.5 67.6 %shard_map.70 = (f32[8,256,1024]{2,1,0:T(8,128)}, bf16[1024,1024]{1,0:T(8,128)(2,1)}) custom-call(s32[8]{0:T(128)} %get-tuple-element.9.slot_ref, s32[8]{0:T(128)} %get-tuple-element.10.used_ref, f32[8,256,1024]{2,1,0:T(8,128)} %bitcast.11, bf16[4,256,1024]{2,1,0:T(8,128)(2,1)} %copy-done.1, bf16[1024,1024]{1,0:T(8,128)(2,1)} %copy-done), custom_call_target="tpu_custom_call" | custom-call | bytes 18874368 | tf_op jit(solution)/shard_map/pallas_call | solution.py:118
Async XLA Ops:
  0.6 5.1 %copy-start.2 = (bf16[1,256,2048]{2,1,0:T(8,128)(2,1)S(1)}, bf16[1,256,2048]{2,1,0:T(8,128)(2,1)}, u32[]{:S(2)}) copy-start(bf16[1,256,2048]{2,1,0:T(8,128)(2,1)} %param.6) | copy-start | bytes 3145732
  0.6 5.0 %copy-start.3 = (bf16[1,256,1024]{2,1,0:T(8,128)(2,1)S(1)}, bf16[1,256,1024]{2,1,0:T(8,128)(2,1)}, u32[]{:S(2)}) copy-start(bf16[1,256,1024]{2,1,0:T(8,128)(2,1)} %param.7) | copy-start | bytes 1572868
  99.9 1.3 copy-start
  101.2 1.4 copy-start.1

commit v3 on v1

--- a/solution.py
+++ b/solution.py
@@ -56,29 +56,17 @@
     return (new_weight[None], new_velocity[:, None])
 
 
-def select_kernel(route_ref, momentum_ref, out_ref):
-    out_ref[...] = momentum_ref[...].astype(out_ref.dtype)
-
-
-def select_momentum(route, momentum):
-    n_path = route.shape[0]
-    _, rows, cols = momentum.shape
-    return pl.pallas_call(
-        select_kernel,
-        out_shape=jax.ShapeDtypeStruct((n_path, rows, cols), jnp.bfloat16),
-        grid_spec=pltpu.PrefetchScalarGridSpec(
-            num_scalar_prefetch=1,
-            grid=(n_path,),
-            in_specs=[pl.BlockSpec((1, rows, cols), lambda p, route: (route[p], 0, 0))],
-            out_specs=pl.BlockSpec((1, rows, cols), lambda p, route: (p, 0, 0)),
-        ),
-        compiler_params=pltpu.CompilerParams(vmem_limit_bytes=32 * 2**20),
-        cost_estimate=pl.CostEstimate(flops=0, bytes_accessed=n_path * rows * cols * 6, transcendentals=0),
-    )(route, momentum)
-
-
-def momentum_kernel(slot_ref, used_ref, momentum_ref, delta_ref, out_ref):
-    used = used_ref[pl.program_id(0)]
+def path_of(route_ref, m):
+    slot, used = jnp.int32(0), jnp.int32(0)
+    for p in range(route_ref.shape[0]):
+        hit = route_ref[p] == m
+        slot = jnp.where(hit, p, slot)
+        used = jnp.where(hit, 1, used)
+    return slot, used
+
+
+def momentum_kernel(route_ref, momentum_ref, delta_ref, out_ref):
+    _, used = path_of(route_ref, pl.program_id(0))
 
     @pl.when(used != 0)
     def _():
@@ -91,35 +79,34 @@
 
 def next_momentum(route, momentum, received):
     modules, rows, cols = momentum.shape
-    hit = route[:, None] == jnp.arange(modules, dtype=jnp.int32)[None, :]
-    used = jnp.any(hit, axis=0).astype(jnp.int32)
-    slot = jnp.argmax(hit, axis=0).astype(jnp.int32)
     return pl.pallas_call(
         momentum_kernel,
         out_shape=jax.ShapeDtypeStruct((modules, rows, cols), jnp.float32),
         grid_spec=pltpu.PrefetchScalarGridSpec(
-            num_scalar_prefetch=2,
+            num_scalar_prefetch=1,
             grid=(modules,),
             in_specs=[
-                pl.BlockSpec((1, rows, cols), lambda m, slot, used: (m, 0, 0)),
-                pl.BlockSpec((1, rows, cols), lambda m, slot, used: (slot[m], 0, 0)),
+                pl.BlockSpec((1, rows, cols), lambda m, route: (m, 0, 0)),
+                pl.BlockSpec((1, rows, cols), lambda m, route: (path_of(route, m)[0], 0, 0)),
             ],
-            out_specs=pl.BlockSpec((1, rows, cols), lambda m, slot, used: (m, 0, 0)),
+            out_specs=pl.BlockSpec((1, rows, cols), lambda m, route: (m, 0, 0)),
         ),
         compiler_params=pltpu.CompilerParams(vmem_limit_bytes=32 * 2**20),
         cost_estimate=pl.CostEstimate(flops=0, bytes_accessed=modules * rows * cols * 9, transcendentals=0),
-    )(slot, used, momentum, received)
+    )(route, momentum, received)
 
 
 def sync_kernel(
     n_path,
     chunks,
+    route_ref,
     x_hbm,
     t_hbm,
     w_hbm,
     m_hbm,
     new_w_hbm,
     recv_hbm,
+    held_hbm,
     x_v,
     t_v,
     w_v,
@@ -131,7 +118,10 @@
     resid,
     delta,
     mom,
+    held,
+    msend,
     load_sem,
+    held_sem,
     out_sem,
     x_send,
     x_recv,
@@ -155,11 +145,20 @@
     load_x = pltpu.make_async_copy(x_hbm, x_v, load_sem.at[0])
     load_w = pltpu.make_async_copy(w_hbm, w_v, load_sem.at[1])
     load_t = pltpu.make_async_copy(t_hbm, t_v, load_sem.at[2])
-    load_m = pltpu.make_async_copy(m_hbm.at[me], mom.at[me], load_sem.at[3])
+    load_m = pltpu.make_async_copy(msend.at[me], mom.at[me], load_sem.at[3])
+    cuts = held_sem.shape[0] // 2
+    strip = block // cuts
+    strips = [pl.ds(c * strip, strip) for c in range(cuts)]
+    take = [pltpu.make_async_copy(m_hbm.at[:, at], held.at[:, at], held_sem.at[c]) for c, at in enumerate(strips)]
+    give = [
+        pltpu.make_async_copy(held.at[:, at], held_hbm.at[:, at], held_sem.at[cuts + c]) for c, at in enumerate(strips)
+    ]
+    take[0].start()
     load_x.start()
+    for copy in take[1:]:
+        copy.start()
     load_w.start()
     load_t.start()
-    load_m.start()
 
     barrier = pltpu.get_barrier_semaphore()
     pl.semaphore_signal(barrier, inc=1, device_id={"inner": other}, device_id_type=pl.DeviceIdType.MESH)
@@ -169,12 +168,12 @@
         )
     pl.semaphore_wait(barrier, n_path)
 
-    def far(d, src, dst, send, recv):
+    def far(d, src, dst, send, recv, c=0):
         return pltpu.make_async_remote_copy(
             src_ref=src,
             dst_ref=dst,
-            send_sem=send.at[d - 1],
-            recv_sem=recv.at[d - 1],
+            send_sem=send.at[c, d - 1],
+            recv_sem=recv.at[c, d - 1],
             device_id={"path": lax.rem(me + d, n_path)},
             device_id_type=pl.DeviceIdType.MESH,
         )
@@ -189,9 +188,26 @@
             device_id_type=pl.DeviceIdType.MESH,
         )
 
-    mom_copies = [far(d, m_hbm.at[lax.rem(me + d, n_path)], mom.at[me], m_send, m_recv) for d in range(1, n_path)]
-    for copy in mom_copies:
-        copy.start()
+    modules = held.shape[0]
+    mom_copies = []
+    for c, at in enumerate(strips):
+        take[c].wait()
+
+        @pl.loop(0, strip // 16)
+        def _(k, c=c):
+            rows_at = pl.ds(pl.multiple_of(c * strip + k * 16, 16), 16)
+            for p in range(n_path):
+                chosen = held[0, rows_at, :]
+                for m in range(1, modules):
+                    chosen = jnp.where(route_ref[p] == m, held[m, rows_at, :], chosen)
+                msend[p, rows_at, :] = chosen.astype(jnp.bfloat16)
+
+        for d in range(1, n_path):
+            copy = far(d, msend.at[lax.rem(me + d, n_path), at], mom.at[me, at], m_send, m_recv, c)
+            copy.start()
+            mom_copies.append((d, copy))
+        give[c].start()
+    load_m.start()
 
     load_x.wait()
     piece = 32
@@ -279,7 +295,9 @@
         if d == 0:
             load_m.wait()
         else:
-            mom_copies[d - 1].wait_recv()
+            for offset, copy in mom_copies:
+                if offset == d:
+                    copy.wait_recv()
         o = lax.rem(me + n_path - d, n_path)
 
         @pl.loop(0, block // piece)
@@ -296,8 +314,10 @@
         copy.start()
         out_copies.append(copy)
 
-    for copy in hop0 + hop1 + hop2 + mom_copies:
+    for copy in hop0 + hop1 + hop2 + [copy for _, copy in mom_copies]:
         copy.wait_send()
+    for copy in give:
+        copy.wait()
     for copy in delta_copies[:-1]:
         copy.wait()
     delta_copies[-1].wait()
@@ -313,17 +333,18 @@
     chunks = 2
     bf16 = jnp.bfloat16
     held = momentum[:, 0]
-    outgoing = select_momentum(route, held)
+    cuts = 4
     any_space = pl.BlockSpec(memory_space=pl.ANY)
     dma = pltpu.SemaphoreType.DMA
-    new_weight, received = pl.pallas_call(
+    new_weight, received, kept = pl.pallas_call(
         functools.partial(sync_kernel, n_path, chunks),
         out_shape=(
             jax.ShapeDtypeStruct((rows, cols), bf16),
             jax.ShapeDtypeStruct((n_path, block, cols), bf16),
+            jax.ShapeDtypeStruct(held.shape, held.dtype),
         ),
-        in_specs=[any_space] * 4,
-        out_specs=(any_space, any_space),
+        in_specs=[pl.BlockSpec(memory_space=pltpu.SMEM)] + [any_space] * 4,
+        out_specs=(any_space,) * 3,
         scratch_shapes=[
             pltpu.VMEM((tokens, width), bf16),
             pltpu.VMEM((tokens, cols), bf16),
@@ -336,23 +357,26 @@
             pltpu.VMEM((2 * tokens, cols), bf16),
             pltpu.VMEM((n_path, block, cols), bf16),
             pltpu.VMEM((n_path, block, cols), bf16),
+            pltpu.VMEM(held.shape, held.dtype),
+            pltpu.VMEM((n_path, block, cols), bf16),
             dma((4,)),
+            dma((2 * cuts,)),
             dma((1 + n_path,)),
             dma((3, chunks)),
             dma((3, chunks)),
-            dma((n_path - 1,)),
-            dma((n_path - 1,)),
-            dma((n_path - 1,)),
-            dma((n_path - 1,)),
+            dma((cuts, n_path - 1)),
+            dma((cuts, n_path - 1)),
+            dma((1, n_path - 1)),
+            dma((1, n_path - 1)),
         ],
         compiler_params=pltpu.CompilerParams(
-            collective_id=0, has_side_effects=True, vmem_limit_bytes=48 * 2**20
+            collective_id=0, has_side_effects=True, vmem_limit_bytes=38 * 2**20
         ),
         cost_estimate=pl.CostEstimate(
             flops=8 * tokens * rows * cols, bytes_accessed=12 * rows * cols, transcendentals=0
         ),
-    )(inputs[0], targets[0], path_weights[0], outgoing)
-    return (new_weight[None], next_momentum(route, held, received)[:, None])
+    )(route, *[pltpu.with_memory_space_constraint(a, pltpu.HBM) for a in (inputs[0], targets[0], path_weights[0], held)])
+    return (new_weight[None], next_momentum(route, kept, received)[:, None])
 
 
 def solution(mesh):

time: 110 us -> 103 us (0.936)
  local copies, waits for them, and re-layouts: 6.68 us -> 1.97 us
  other arithmetic: 2.01 us -> 0 us
    unnamed x13 -> x3, local copies, waits for them, and re-layouts: 6.68 us -> 1.97 us
    another operation x1 -> x0, other arithmetic: 1.26 us -> none  [next_momentum(): slot = jnp.argmax(hit, axis=0).astype(jnp.int32)]
where the time goes in v3:
time: 103 us
  Pallas kernels  100 us (97%)
  local copies, waits for them, and re-layouts  1.97 us (2%)
    pallas_call x1, Pallas kernels, distinct_device(): pl.pallas_call(functools.partial(sync_kernel, n_path, chunks), out_shape=...  95.2 us
    pallas_call x1, Pallas kernels, next_momentum(): pl.pallas_call(momentum_kernel, out_shape=jax.ShapeDtypeStruct((modules,...  5.19 us

profile of v3, /device:TPU:8, one launch (start us, length us, event | category | flops | bytes accessed | tf_op | source)
XLA Modules:
  0.0 103.0 jit_solution(1337948888522765230)
XLA Ops:
  0.6 0.0 copy-start
  0.6 0.6 copy-done
  1.3 95.2 %shard_map.68 = (bf16[1024,1024]{1,0:T(8,128)(2,1)S(1)}, bf16[4,256,1024]{2,1,0:T(8,128)(2,1)S(1)}, f32[8,256,1024]{2,1,0:T(8,128)S(1)}) custom-call(s32[4]{0:T(128)S(1)} %copy-done, bf16[256,2048]{1,0:T(8,128)(2,1)} %bitcast.12, bf16[256,1024]{1,0:T(8,128)(2,1)} %bitcast.13, bf16[1024,1024]{1,0:T(8,128)(2,1)} %bitcast.11, f32[8,256,1024]{2,1,0:T(8,128)} %bitcast.9), custom_call_target="tpu_custom_call" | custom-call | flops 2147483648 | bytes 12582912 | tf_op jit(solution)/shard_map/pallas_call | solution.py:339
  96.5 5.2 %shard_map.69 = f32[8,256,1024]{2,1,0:T(8,128)} custom-call(s32[4]{0:T(128)S(1)} %copy-done, f32[8,256,1024]{2,1,0:T(8,128)S(1)} %get-tuple-element.6.momentum_ref, bf16[4,256,1024]{2,1,0:T(8,128)(2,1)S(1)} %get-tuple-element.7.delta_ref), custom_call_target="tpu_custom_call" | custom-call | bytes 18874368 | tf_op jit(solution)/shard_map/pallas_call | solution.py:82
  101.7 1.3 %copy.9 = bf16[1,1024,1024]{2,1,0:T(8,128)(2,1)} copy(bf16[1,1024,1024]{2,1,0:T(8,128)(2,1)S(1)} %bitcast.8) | data formatting | bytes 4194304
Async XLA Ops:
  0.6 0.7 copy-start

commit v4 on v3

--- a/solution.py
+++ b/solution.py
@@ -56,44 +56,31 @@
     return (new_weight[None], new_velocity[:, None])
 
 
-def path_of(route_ref, m):
-    slot, used = jnp.int32(0), jnp.int32(0)
-    for p in range(route_ref.shape[0]):
-        hit = route_ref[p] == m
-        slot = jnp.where(hit, p, slot)
-        used = jnp.where(hit, 1, used)
-    return slot, used
-
-
-def momentum_kernel(route_ref, momentum_ref, delta_ref, out_ref):
-    _, used = path_of(route_ref, pl.program_id(0))
-
-    @pl.when(used != 0)
-    def _():
-        out_ref[...] = outer_mu * momentum_ref[...] + delta_ref[...].astype(jnp.float32)
-
-    @pl.when(used == 0)
-    def _():
-        out_ref[...] = outer_mu * momentum_ref[...]
-
-
-def next_momentum(route, momentum, received):
-    modules, rows, cols = momentum.shape
+def momentum_kernel(route_ref, decayed_ref, delta_ref, weight_ref, out_ref, new_weight_ref):
+    out_ref[...] = decayed_ref[...] + delta_ref[...].astype(jnp.float32)
+
+
+def next_momentum(route, decayed, received, new_weight):
+    modules, rows, cols = decayed.shape
+    n_path = received.shape[0]
+    module = pl.BlockSpec((1, rows, cols), lambda p, route: (route[p], 0, 0))
+    whole = pl.BlockSpec(memory_space=pl.ANY)
     return pl.pallas_call(
         momentum_kernel,
-        out_shape=jax.ShapeDtypeStruct((modules, rows, cols), jnp.float32),
+        out_shape=(
+            jax.ShapeDtypeStruct((modules, rows, cols), jnp.float32),
+            jax.ShapeDtypeStruct(new_weight.shape, new_weight.dtype),
+        ),
         grid_spec=pltpu.PrefetchScalarGridSpec(
             num_scalar_prefetch=1,
-            grid=(modules,),
-            in_specs=[
-                pl.BlockSpec((1, rows, cols), lambda m, route: (m, 0, 0)),
-                pl.BlockSpec((1, rows, cols), lambda m, route: (path_of(route, m)[0], 0, 0)),
-            ],
-            out_specs=pl.BlockSpec((1, rows, cols), lambda m, route: (m, 0, 0)),
-        ),
+            grid=(n_path,),
+            in_specs=[module, pl.BlockSpec((1, rows, cols), lambda p, route: (p, 0, 0)), whole],
+            out_specs=(module, whole),
+        ),
+        input_output_aliases={1: 0, 3: 1},
         compiler_params=pltpu.CompilerParams(vmem_limit_bytes=32 * 2**20),
-        cost_estimate=pl.CostEstimate(flops=0, bytes_accessed=modules * rows * cols * 9, transcendentals=0),
-    )(route, momentum, received)
+        cost_estimate=pl.CostEstimate(flops=0, bytes_accessed=n_path * rows * cols * 10, transcendentals=0),
+    )(route, decayed, received, new_weight)
 
 
 def sync_kernel(
@@ -201,6 +188,7 @@
                 for m in range(1, modules):
                     chosen = jnp.where(route_ref[p] == m, held[m, rows_at, :], chosen)
                 msend[p, rows_at, :] = chosen.astype(jnp.bfloat16)
+            held[:, rows_at, :] = outer_mu * held[:, rows_at, :]
 
         for d in range(1, n_path):
             copy = far(d, msend.at[lax.rem(me + d, n_path), at], mom.at[me, at], m_send, m_recv, c)
@@ -333,6 +321,7 @@
     chunks = 2
     bf16 = jnp.bfloat16
     held = momentum[:, 0]
+    route = pltpu.with_memory_space_constraint(route, pltpu.HBM)
     cuts = 4
     any_space = pl.BlockSpec(memory_space=pl.ANY)
     dma = pltpu.SemaphoreType.DMA
@@ -376,7 +365,8 @@
             flops=8 * tokens * rows * cols, bytes_accessed=12 * rows * cols, transcendentals=0
         ),
     )(route, *[pltpu.with_memory_space_constraint(a, pltpu.HBM) for a in (inputs[0], targets[0], path_weights[0], held)])
-    return (new_weight[None], next_momentum(route, kept, received)[:, None])
+    velocity, new_weight = next_momentum(route, kept, received, new_weight)
+    return (new_weight[None], velocity[:, None])
 
 
 def solution(mesh):

time: 103 us -> 102 us (level)
  Pallas kernels: 100 us -> 96.8 us
  local copies, waits for them, and re-layouts: 1.97 us -> 4.72 us
    pallas_call x1, Pallas kernels: 5.19 us -> 1.3 us  [next_momentum(): pl.pallas_call(momentum_kernel, out_shape=(jax.ShapeDtypeStruct((modules,...]
    unnamed x3 -> x2, local copies, waits for them, and re-layouts: 1.97 us -> 4.72 us
where the time goes in v4:
time: 102 us
  Pallas kernels  96.8 us (95%)
  local copies, waits for them, and re-layouts  4.72 us (5%)
    pallas_call x1, Pallas kernels, distinct_device(): pl.pallas_call(functools.partial(sync_kernel, n_path, chunks), out_shape=...  95.5 us
    unnamed x2, local copies, waits for them, and re-layouts  4.72 us

profile of v4, /device:TPU:8, one launch (start us, length us, event | category | flops | bytes accessed | tf_op | source)
XLA Modules:
  0.0 102.2 jit_solution(1632325366019203171)
XLA Ops:
  0.6 95.5 %shard_map.68 = (bf16[1024,1024]{1,0:T(8,128)(2,1)S(1)}, bf16[4,256,1024]{2,1,0:T(8,128)(2,1)S(1)}, f32[8,256,1024]{2,1,0:T(8,128)S(1)}) custom-call(s32[4]{0:T(128)} %route_ref.3, bf16[256,2048]{1,0:T(8,128)(2,1)} %bitcast.12, bf16[256,1024]{1,0:T(8,128)(2,1)} %bitcast.13, bf16[1024,1024]{1,0:T(8,128)(2,1)} %bitcast.11, f32[8,256,1024]{2,1,0:T(8,128)} %bitcast.10), custom_call_target="tpu_custom_call" | custom-call | flops 2147483648 | bytes 12582912 | tf_op jit(solution)/shard_map/pallas_call | solution.py:328
  96.2 1.3 %shard_map.69 = (f32[8,256,1024]{2,1,0:T(8,128)S(1)}, bf16[1024,1024]{1,0:T(8,128)(2,1)S(1)}) custom-call(s32[4]{0:T(128)} %route_ref.3, f32[8,256,1024]{2,1,0:T(8,128)S(1)} %get-tuple-element.7.decayed_ref, bf16[4,256,1024]{2,1,0:T(8,128)(2,1)S(1)} %get-tuple-element.8.delta_ref, ...), custom_call_target="tpu_custom_call", output_to_operand_aliasing={{0}: (1, {}), {1}: (3, {})} | custom-call | bytes 10485760 | tf_op jit(solution)/shard_map/pallas_call | solution.py:68
  97.5 1.3 %copy.14 = bf16[1,1024,1024]{2,1,0:T(8,128)(2,1)} copy(bf16[1,1024,1024]{2,1,0:T(8,128)(2,1)S(1)} %bitcast.9) | data formatting | bytes 4194304
  98.8 3.4 %copy.15 = f32[8,1,256,1024]{3,2,1,0:T(8,128)} copy(f32[8,1,256,1024]{3,2,1,0:T(8,128)S(1)} %bitcast.8) | data formatting | bytes 16777216

commit v5 on v4

--- a/solution.py
+++ b/solution.py
@@ -322,7 +322,7 @@
     bf16 = jnp.bfloat16
     held = momentum[:, 0]
     route = pltpu.with_memory_space_constraint(route, pltpu.HBM)
-    cuts = 4
+    cuts = 8
     any_space = pl.BlockSpec(memory_space=pl.ANY)
     dma = pltpu.SemaphoreType.DMA
     new_weight, received, kept = pl.pallas_call(

time: 102 us -> 102 us (level)
  no operation moved by 1% of the time
where the time goes in v5:
time: 102 us
  Pallas kernels  96.6 us (95%)
  local copies, waits for them, and re-layouts  4.72 us (5%)
    pallas_call x1, Pallas kernels, distinct_device(): pl.pallas_call(functools.partial(sync_kernel, n_path, chunks), out_shape=...  95.3 us
    unnamed x2, local copies, waits for them, and re-layouts  4.72 us

profile of v5, /device:TPU:8, one launch (start us, length us, event | category | flops | bytes accessed | tf_op | source)
XLA Modules:
  0.0 102.0 jit_solution(18131665492185959688)
XLA Ops:
  0.6 95.3 %shard_map.68 = (bf16[1024,1024]{1,0:T(8,128)(2,1)S(1)}, bf16[4,256,1024]{2,1,0:T(8,128)(2,1)S(1)}, f32[8,256,1024]{2,1,0:T(8,128)S(1)}) custom-call(s32[4]{0:T(128)} %route_ref.3, bf16[256,2048]{1,0:T(8,128)(2,1)} %bitcast.12, bf16[256,1024]{1,0:T(8,128)(2,1)} %bitcast.13, bf16[1024,1024]{1,0:T(8,128)(2,1)} %bitcast.11, f32[8,256,1024]{2,1,0:T(8,128)} %bitcast.10), custom_call_target="tpu_custom_call" | custom-call | flops 2147483648 | bytes 12582912 | tf_op jit(solution)/shard_map/pallas_call | solution.py:328
  95.9 1.3 %shard_map.69 = (f32[8,256,1024]{2,1,0:T(8,128)S(1)}, bf16[1024,1024]{1,0:T(8,128)(2,1)S(1)}) custom-call(s32[4]{0:T(128)} %route_ref.3, f32[8,256,1024]{2,1,0:T(8,128)S(1)} %get-tuple-element.7.decayed_ref, bf16[4,256,1024]{2,1,0:T(8,128)(2,1)S(1)} %get-tuple-element.8.delta_ref, ...), custom_call_target="tpu_custom_call", output_to_operand_aliasing={{0}: (1, {}), {1}: (3, {})} | custom-call | bytes 10485760 | tf_op jit(solution)/shard_map/pallas_call | solution.py:68
  97.2 1.3 %copy.14 = bf16[1,1024,1024]{2,1,0:T(8,128)(2,1)} copy(bf16[1,1024,1024]{2,1,0:T(8,128)(2,1)S(1)} %bitcast.9) | data formatting | bytes 4194304
  98.6 3.4 %copy.15 = f32[8,1,256,1024]{3,2,1,0:T(8,128)} copy(f32[8,1,256,1024]{3,2,1,0:T(8,128)S(1)} %bitcast.8) | data formatting | bytes 16777216
